TPU v7x, 256 devices: a whole 4x4x8 slice. The times are simulated.
256 devices in a mesh: blk: 16 (over z, x_hi), group: 16 (over x_lo, y, core).
Axes of the slice: x: 4 (x_hi: 2, x_lo: 2; x = x_hi * 2 + x_lo), y: 4, z: 8, core: 2. Of those that a mesh axis runs over, the one named last changes fastest.
Arguments:
- images: float32 [262144, 1024], P(('blk', 'group')), may hold values from -0.1875 to 0.1875
- texts: float32 [2048, 1024], P(('blk', 'group')), may hold values from -0.1875 to 0.1875
- row_lse: float32 [262144], P(('blk', 'group')), may hold values from 12 to 14
- row_weights: float32 [262144], P(('blk', 'group')), may hold values from 0.3 to 3
- pair_ids: int32 [262144], P(('blk', 'group')), may hold values from 0 to 2047
Outputs:
- image_grads: float32 [262144, 1024], P(('blk', 'group'))
- text_grads: float32 [2048, 1024], P(('blk', 'group'))
All inputs are finite; a program needn't handle non-finite values.
Results may differ from a plain program's by a relative error of at most 0.011.
Values may be sent and summed in bfloat16 or wider, within the bound.
A program may use at most 64 MiB of HBM per device.

v0:
```python
import jax
import jax.numpy as jnp
from jax import lax
from jax.sharding import PartitionSpec as P

logit_scale = 100.0


def shifted(block, axis, distance):
    devices = range(lax.axis_size(axis))
    route = [((i - distance) % len(devices), i) for i in devices]
    return lax.ppermute(block, axis, route)


def shards(images, texts, row_lse, row_weights, pair_ids):
    blocks = lax.axis_size("blk")
    members = lax.axis_size("group")
    here = lax.axis_index("blk")
    rows = texts.shape[0]
    panel_rows = rows * members
    image_low = images.astype(jnp.bfloat16)

    def tile(panel, anchor):
        columns = anchor * panel_rows + jnp.arange(panel_rows, dtype=jnp.int32)
        scores = jnp.einsum("rd,td->rt", image_low, panel, preferred_element_type=jnp.float32)
        match = (pair_ids[:, None] == columns[None, :]).astype(jnp.float32)
        coeffs = row_weights[:, None] * (jnp.exp(logit_scale * scores - row_lse[:, None]) - match)
        coeffs = coeffs.astype(jnp.bfloat16)
        grads = logit_scale * jnp.dot(coeffs, panel, preferred_element_type=jnp.float32)
        return (coeffs, grads)

    start_grads = jnp.zeros(images.shape, jnp.float32)

    def turn(step, carry):
        shard, summed, image_grads = carry
        anchor = (here - step) % blocks
        panel = lax.all_gather(shard.astype(jnp.bfloat16), "group", axis=0, tiled=True)
        coeffs, grads = tile(panel, anchor)
        reduced = lax.psum_scatter(
            logit_scale
            * jnp.einsum("rt,rd->td", coeffs, image_low, preferred_element_type=jnp.float32),
            "group",
            scatter_dimension=0,
            tiled=True,
        )
        shard, summed = shifted((shard, summed + reduced), "blk", 1)
        return (shard, summed, image_grads + grads)

    start = (texts, jnp.zeros(texts.shape, jnp.float32), start_grads)
    shard, text_grads, image_grads = lax.fori_loop(0, blocks, turn, start)
    return (image_grads, text_grads)


def solution(mesh):
    placed = (
        P(("blk", "group"), None),
        P(("blk", "group"), None),
        P(("blk", "group")),
        P(("blk", "group")),
        P(("blk", "group")),
    )
    return jax.shard_map(
        shards,
        mesh=mesh,
        in_specs=placed,
        out_specs=(P(("blk", "group"), None), P(("blk", "group"), None)),
        check_vma=False,
    )
```

profile of v0, /device:TPU:8, one launch (start us, length us, event | category | flops | bytes accessed | tf_op | source)
XLA Modules:
  0.0 1437.7 jit_solution(14413211364907691934)
XLA Ops:
  10.5 1420.0 %while.20 = (s32[]{:T(128)}, bf16[8,1024]{1,0:T(8,128)(2,1)S(1)}, f32[8,1024]{1,0:T(8,128)S(1)}, f32[1024,1024]{1,0:T(8,128)}, f32[1024]{0:T(1024)S(1)}, /*index...) while((s32[]{:T(128)}, bf16[8,1024]{1,0:T(8,128)(2,1)S(1)}, ...), condition=%wide.region_2.3_spmd.clone, body=%wide.region_0.2_spmd.clone.sunk | while | flops 809508992 | bytes 16709008 | solution.py:50
  10.6 18.8 %all_gather.12 = bf16[128,1024]{1,0:T(8,128)(2,1)S(1)} all-gather(bf16[8,1024]{1,0:T(8,128)(2,1)S(1)} %copy.12), channel_id=1, replica_groups=mesh['blk'=16,'group'=16] {'group'}, dimensions={0}, use_global_device_ids=true | all-gather | bytes 278528 | tf_op jit(solution)/shard_map/while/body/eval_jaxpr/all_gather | solution.py:37
  33.1 59.5 %reduce-scatter.2.cloned.1.call-done = f32[8,1024]{1,0:T(8,128)} async-done(((f32[128,1024]{1,0:T(8,128)}), f32[8,1024]{1,0:T(8,128)}) %reduce-scatter.2.cloned.1.call-update) | async-done | bytes 32784 | tf_op jit(solution)/shard_map/while/body/eval_jaxpr/reduce_scatter | solution.py:39
  93.4 2.7 collective-permute-start.1
  96.1 2.7 select_add_fusion.2
  100.9 21.0 %all_gather.12 = bf16[128,1024]{1,0:T(8,128)(2,1)S(1)} all-gather(bf16[8,1024]{1,0:T(8,128)(2,1)S(1)} %copy.12), channel_id=1, replica_groups=mesh['blk'=16,'group'=16] {'group'}, dimensions={0}, use_global_device_ids=true | all-gather | bytes 278528 | tf_op jit(solution)/shard_map/while/body/eval_jaxpr/all_gather | solution.py:37
  124.7 56.1 %reduce-scatter.2.cloned.1.call-done = f32[8,1024]{1,0:T(8,128)} async-done(((f32[128,1024]{1,0:T(8,128)}), f32[8,1024]{1,0:T(8,128)}) %reduce-scatter.2.cloned.1.call-update) | async-done | bytes 32784 | tf_op jit(solution)/shard_map/while/body/eval_jaxpr/reduce_scatter | solution.py:39
  181.5 2.7 collective-permute-start.1
  184.2 4.9 select_add_fusion.2
  189.2 21.1 %all_gather.12 = bf16[128,1024]{1,0:T(8,128)(2,1)S(1)} all-gather(bf16[8,1024]{1,0:T(8,128)(2,1)S(1)} %copy.12), channel_id=1, replica_groups=mesh['blk'=16,'group'=16] {'group'}, dimensions={0}, use_global_device_ids=true | all-gather | bytes 278528 | tf_op jit(solution)/shard_map/while/body/eval_jaxpr/all_gather | solution.py:37
  214.2 55.2 %reduce-scatter.2.cloned.1.call-done = f32[8,1024]{1,0:T(8,128)} async-done(((f32[128,1024]{1,0:T(8,128)}), f32[8,1024]{1,0:T(8,128)}) %reduce-scatter.2.cloned.1.call-update) | async-done | bytes 32784 | tf_op jit(solution)/shard_map/while/body/eval_jaxpr/reduce_scatter | solution.py:39
  270.2 2.7 collective-permute-start.1
  272.9 4.9 select_add_fusion.2
  277.9 21.1 %all_gather.12 = bf16[128,1024]{1,0:T(8,128)(2,1)S(1)} all-gather(bf16[8,1024]{1,0:T(8,128)(2,1)S(1)} %copy.12), channel_id=1, replica_groups=mesh['blk'=16,'group'=16] {'group'}, dimensions={0}, use_global_device_ids=true | all-gather | bytes 278528 | tf_op jit(solution)/shard_map/while/body/eval_jaxpr/all_gather | solution.py:37
  302.9 55.2 %reduce-scatter.2.cloned.1.call-done = f32[8,1024]{1,0:T(8,128)} async-done(((f32[128,1024]{1,0:T(8,128)}), f32[8,1024]{1,0:T(8,128)}) %reduce-scatter.2.cloned.1.call-update) | async-done | bytes 32784 | tf_op jit(solution)/shard_map/while/body/eval_jaxpr/reduce_scatter | solution.py:39
  358.9 2.7 collective-permute-start.1
  361.6 4.9 select_add_fusion.2
  366.5 21.1 %all_gather.12 = bf16[128,1024]{1,0:T(8,128)(2,1)S(1)} all-gather(bf16[8,1024]{1,0:T(8,128)(2,1)S(1)} %copy.12), channel_id=1, replica_groups=mesh['blk'=16,'group'=16] {'group'}, dimensions={0}, use_global_device_ids=true | all-gather | bytes 278528 | tf_op jit(solution)/shard_map/while/body/eval_jaxpr/all_gather | solution.py:37
  391.6 55.2 %reduce-scatter.2.cloned.1.call-done = f32[8,1024]{1,0:T(8,128)} async-done(((f32[128,1024]{1,0:T(8,128)}), f32[8,1024]{1,0:T(8,128)}) %reduce-scatter.2.cloned.1.call-update) | async-done | bytes 32784 | tf_op jit(solution)/shard_map/while/body/eval_jaxpr/reduce_scatter | solution.py:39
  447.5 2.7 collective-permute-start.1
  450.2 4.9 select_add_fusion.2
  455.2 21.1 %all_gather.12 = bf16[128,1024]{1,0:T(8,128)(2,1)S(1)} all-gather(bf16[8,1024]{1,0:T(8,128)(2,1)S(1)} %copy.12), channel_id=1, replica_groups=mesh['blk'=16,'group'=16] {'group'}, dimensions={0}, use_global_device_ids=true | all-gather | bytes 278528 | tf_op jit(solution)/shard_map/while/body/eval_jaxpr/all_gather | solution.py:37
  480.2 55.2 %reduce-scatter.2.cloned.1.call-done = f32[8,1024]{1,0:T(8,128)} async-done(((f32[128,1024]{1,0:T(8,128)}), f32[8,1024]{1,0:T(8,128)}) %reduce-scatter.2.cloned.1.call-update) | async-done | bytes 32784 | tf_op jit(solution)/shard_map/while/body/eval_jaxpr/reduce_scatter | solution.py:39
  536.2 2.7 collective-permute-start.1
  538.9 4.9 select_add_fusion.2
  543.9 21.1 %all_gather.12 = bf16[128,1024]{1,0:T(8,128)(2,1)S(1)} all-gather(bf16[8,1024]{1,0:T(8,128)(2,1)S(1)} %copy.12), channel_id=1, replica_groups=mesh['blk'=16,'group'=16] {'group'}, dimensions={0}, use_global_device_ids=true | all-gather | bytes 278528 | tf_op jit(solution)/shard_map/while/body/eval_jaxpr/all_gather | solution.py:37
  568.9 55.2 %reduce-scatter.2.cloned.1.call-done = f32[8,1024]{1,0:T(8,128)} async-done(((f32[128,1024]{1,0:T(8,128)}), f32[8,1024]{1,0:T(8,128)}) %reduce-scatter.2.cloned.1.call-update) | async-done | bytes 32784 | tf_op jit(solution)/shard_map/while/body/eval_jaxpr/reduce_scatter | solution.py:39
  624.9 2.7 collective-permute-start.1
  627.6 4.9 select_add_fusion.2
  632.6 21.1 %all_gather.12 = bf16[128,1024]{1,0:T(8,128)(2,1)S(1)} all-gather(bf16[8,1024]{1,0:T(8,128)(2,1)S(1)} %copy.12), channel_id=1, replica_groups=mesh['blk'=16,'group'=16] {'group'}, dimensions={0}, use_global_device_ids=true | all-gather | bytes 278528 | tf_op jit(solution)/shard_map/while/body/eval_jaxpr/all_gather | solution.py:37
  657.6 55.2 %reduce-scatter.2.cloned.1.call-done = f32[8,1024]{1,0:T(8,128)} async-done(((f32[128,1024]{1,0:T(8,128)}), f32[8,1024]{1,0:T(8,128)}) %reduce-scatter.2.cloned.1.call-update) | async-done | bytes 32784 | tf_op jit(solution)/shard_map/while/body/eval_jaxpr/reduce_scatter | solution.py:39
  713.5 2.7 collective-permute-start.1
  716.2 4.9 select_add_fusion.2
  721.2 21.1 %all_gather.12 = bf16[128,1024]{1,0:T(8,128)(2,1)S(1)} all-gather(bf16[8,1024]{1,0:T(8,128)(2,1)S(1)} %copy.12), channel_id=1, replica_groups=mesh['blk'=16,'group'=16] {'group'}, dimensions={0}, use_global_device_ids=true | all-gather | bytes 278528 | tf_op jit(solution)/shard_map/while/body/eval_jaxpr/all_gather | solution.py:37
  746.2 55.2 %reduce-scatter.2.cloned.1.call-done = f32[8,1024]{1,0:T(8,128)} async-done(((f32[128,1024]{1,0:T(8,128)}), f32[8,1024]{1,0:T(8,128)}) %reduce-scatter.2.cloned.1.call-update) | async-done | bytes 32784 | tf_op jit(solution)/shard_map/while/body/eval_jaxpr/reduce_scatter | solution.py:39
  802.2 2.7 collective-permute-start.1
  804.9 4.9 select_add_fusion.2
  809.9 21.1 %all_gather.12 = bf16[128,1024]{1,0:T(8,128)(2,1)S(1)} all-gather(bf16[8,1024]{1,0:T(8,128)(2,1)S(1)} %copy.12), channel_id=1, replica_groups=mesh['blk'=16,'group'=16] {'group'}, dimensions={0}, use_global_device_ids=true | all-gather | bytes 278528 | tf_op jit(solution)/shard_map/while/body/eval_jaxpr/all_gather | solution.py:37
  834.9 55.3 %reduce-scatter.2.cloned.1.call-done = f32[8,1024]{1,0:T(8,128)} async-done(((f32[128,1024]{1,0:T(8,128)}), f32[8,1024]{1,0:T(8,128)}) %reduce-scatter.2.cloned.1.call-update) | async-done | bytes 32784 | tf_op jit(solution)/shard_map/while/body/eval_jaxpr/reduce_scatter | solution.py:39
  890.9 2.7 collective-permute-start.1
  893.6 4.9 select_add_fusion.2
  898.6 21.1 %all_gather.12 = bf16[128,1024]{1,0:T(8,128)(2,1)S(1)} all-gather(bf16[8,1024]{1,0:T(8,128)(2,1)S(1)} %copy.12), channel_id=1, replica_groups=mesh['blk'=16,'group'=16] {'group'}, dimensions={0}, use_global_device_ids=true | all-gather | bytes 278528 | tf_op jit(solution)/shard_map/while/body/eval_jaxpr/all_gather | solution.py:37
  923.6 55.2 %reduce-scatter.2.cloned.1.call-done = f32[8,1024]{1,0:T(8,128)} async-done(((f32[128,1024]{1,0:T(8,128)}), f32[8,1024]{1,0:T(8,128)}) %reduce-scatter.2.cloned.1.call-update) | async-done | bytes 32784 | tf_op jit(solution)/shard_map/while/body/eval_jaxpr/reduce_scatter | solution.py:39
  979.6 2.7 collective-permute-start.1
  982.2 4.9 select_add_fusion.2
  987.2 21.1 %all_gather.12 = bf16[128,1024]{1,0:T(8,128)(2,1)S(1)} all-gather(bf16[8,1024]{1,0:T(8,128)(2,1)S(1)} %copy.12), channel_id=1, replica_groups=mesh['blk'=16,'group'=16] {'group'}, dimensions={0}, use_global_device_ids=true | all-gather | bytes 278528 | tf_op jit(solution)/shard_map/while/body/eval_jaxpr/all_gather | solution.py:37
  1012.3 55.3 %reduce-scatter.2.cloned.1.call-done = f32[8,1024]{1,0:T(8,128)} async-done(((f32[128,1024]{1,0:T(8,128)}), f32[8,1024]{1,0:T(8,128)}) %reduce-scatter.2.cloned.1.call-update) | async-done | bytes 32784 | tf_op jit(solution)/shard_map/while/body/eval_jaxpr/reduce_scatter | solution.py:39
  1068.3 2.7 collective-permute-start.1
  1070.9 4.9 select_add_fusion.2
  1075.9 21.1 %all_gather.12 = bf16[128,1024]{1,0:T(8,128)(2,1)S(1)} all-gather(bf16[8,1024]{1,0:T(8,128)(2,1)S(1)} %copy.12), channel_id=1, replica_groups=mesh['blk'=16,'group'=16] {'group'}, dimensions={0}, use_global_device_ids=true | all-gather | bytes 278528 | tf_op jit(solution)/shard_map/while/body/eval_jaxpr/all_gather | solution.py:37
  1100.9 55.3 %reduce-scatter.2.cloned.1.call-done = f32[8,1024]{1,0:T(8,128)} async-done(((f32[128,1024]{1,0:T(8,128)}), f32[8,1024]{1,0:T(8,128)}) %reduce-scatter.2.cloned.1.call-update) | async-done | bytes 32784 | tf_op jit(solution)/shard_map/while/body/eval_jaxpr/reduce_scatter | solution.py:39
  1156.9 2.7 collective-permute-start.1
  1159.6 4.9 select_add_fusion.2
  1164.6 21.0 %all_gather.12 = bf16[128,1024]{1,0:T(8,128)(2,1)S(1)} all-gather(bf16[8,1024]{1,0:T(8,128)(2,1)S(1)} %copy.12), channel_id=1, replica_groups=mesh['blk'=16,'group'=16] {'group'}, dimensions={0}, use_global_device_ids=true | all-gather | bytes 278528 | tf_op jit(solution)/shard_map/while/body/eval_jaxpr/all_gather | solution.py:37
  1189.6 55.3 %reduce-scatter.2.cloned.1.call-done = f32[8,1024]{1,0:T(8,128)} async-done(((f32[128,1024]{1,0:T(8,128)}), f32[8,1024]{1,0:T(8,128)}) %reduce-scatter.2.cloned.1.call-update) | async-done | bytes 32784 | tf_op jit(solution)/shard_map/while/body/eval_jaxpr/reduce_scatter | solution.py:39
  1248.3 4.9 select_add_fusion.2
  1253.3 21.1 %all_gather.12 = bf16[128,1024]{1,0:T(8,128)(2,1)S(1)} all-gather(bf16[8,1024]{1,0:T(8,128)(2,1)S(1)} %copy.12), channel_id=1, replica_groups=mesh['blk'=16,'group'=16] {'group'}, dimensions={0}, use_global_device_ids=true | all-gather | bytes 278528 | tf_op jit(solution)/shard_map/while/body/eval_jaxpr/all_gather | solution.py:37
  1278.3 55.2 %reduce-scatter.2.cloned.1.call-done = f32[8,1024]{1,0:T(8,128)} async-done(((f32[128,1024]{1,0:T(8,128)}), f32[8,1024]{1,0:T(8,128)}) %reduce-scatter.2.cloned.1.call-update) | async-done | bytes 32784 | tf_op jit(solution)/shard_map/while/body/eval_jaxpr/reduce_scatter | solution.py:39
  1334.3 2.7 collective-permute-start.1
  1337.0 4.9 select_add_fusion.2
  1342.0 21.0 %all_gather.12 = bf16[128,1024]{1,0:T(8,128)(2,1)S(1)} all-gather(bf16[8,1024]{1,0:T(8,128)(2,1)S(1)} %copy.12), channel_id=1, replica_groups=mesh['blk'=16,'group'=16] {'group'}, dimensions={0}, use_global_device_ids=true | all-gather | bytes 278528 | tf_op jit(solution)/shard_map/while/body/eval_jaxpr/all_gather | solution.py:37
  1366.9 55.2 %reduce-scatter.2.cloned.1.call-done = f32[8,1024]{1,0:T(8,128)} async-done(((f32[128,1024]{1,0:T(8,128)}), f32[8,1024]{1,0:T(8,128)}) %reduce-scatter.2.cloned.1.call-update) | async-done | bytes 32784 | tf_op jit(solution)/shard_map/while/body/eval_jaxpr/reduce_scatter | solution.py:39
  1422.9 2.7 collective-permute-start.1
  1425.6 4.9 select_add_fusion.2
  (172 shorter events, 82.9 us)
Async XLA Ops:
  7.2 3.3 copy-start.2
  7.2 3.3 copy-start
  7.2 3.3 copy-start.1
  10.6 82.1 %reduce-scatter.2.cloned.1.call-start = ((), (), s32[]{:S(2)}) async-start(), calls=%async_computation.1 | async-start | bytes 557056 | tf_op jit(solution)/shard_map/while/body/eval_jaxpr/reduce_scatter | solution.py:39
  31.5 67.3 %collective-permute-start = (bf16[8,1024]{1,0:T(8,128)(2,1)S(1)}, bf16[8,1024]{1,0:T(8,128)(2,1)S(1)}, u32[]{:S(2)}, u32[]{:S(2)}) collective-permute-start(bf16[8,1024]{1,0:T(8,128)(2,1)S(1)} %copy.12), channel_id=1, source_target_pairs={{240,0},{0,16},{16,32},{32,48},{48,64},{64,80},{80,96},{96,112},{1... | collective-permute-start | bytes 49160 | tf_op jit(solution)/shard_map/while/body/eval_jaxpr/ppermute | solution.py:12
  93.4 7.5 collective-permute-start.1
  100.9 79.9 %reduce-scatter.2.cloned.1.call-start = ((), (), s32[]{:S(2)}) async-start(), calls=%async_computation.1 | async-start | bytes 557056 | tf_op jit(solution)/shard_map/while/body/eval_jaxpr/reduce_scatter | solution.py:39
  124.0 65.1 %collective-permute-start = (bf16[8,1024]{1,0:T(8,128)(2,1)S(1)}, bf16[8,1024]{1,0:T(8,128)(2,1)S(1)}, u32[]{:S(2)}, u32[]{:S(2)}) collective-permute-start(bf16[8,1024]{1,0:T(8,128)(2,1)S(1)} %copy.12), channel_id=1, source_target_pairs={{240,0},{0,16},{16,32},{32,48},{48,64},{64,80},{80,96},{96,112},{1... | collective-permute-start | bytes 49160 | tf_op jit(solution)/shard_map/while/body/eval_jaxpr/ppermute | solution.py:12
  181.5 7.6 collective-permute-start.1
  189.1 80.3 %reduce-scatter.2.cloned.1.call-start = ((), (), s32[]{:S(2)}) async-start(), calls=%async_computation.1 | async-start | bytes 557056 | tf_op jit(solution)/shard_map/while/body/eval_jaxpr/reduce_scatter | solution.py:39
  212.3 65.5 %collective-permute-start = (bf16[8,1024]{1,0:T(8,128)(2,1)S(1)}, bf16[8,1024]{1,0:T(8,128)(2,1)S(1)}, u32[]{:S(2)}, u32[]{:S(2)}) collective-permute-start(bf16[8,1024]{1,0:T(8,128)(2,1)S(1)} %copy.12), channel_id=1, source_target_pairs={{240,0},{0,16},{16,32},{32,48},{48,64},{64,80},{80,96},{96,112},{1... | collective-permute-start | bytes 49160 | tf_op jit(solution)/shard_map/while/body/eval_jaxpr/ppermute | solution.py:12
  270.2 7.6 collective-permute-start.1
  277.8 80.3 %reduce-scatter.2.cloned.1.call-start = ((), (), s32[]{:S(2)}) async-start(), calls=%async_computation.1 | async-start | bytes 557056 | tf_op jit(solution)/shard_map/while/body/eval_jaxpr/reduce_scatter | solution.py:39
  300.9 65.5 %collective-permute-start = (bf16[8,1024]{1,0:T(8,128)(2,1)S(1)}, bf16[8,1024]{1,0:T(8,128)(2,1)S(1)}, u32[]{:S(2)}, u32[]{:S(2)}) collective-permute-start(bf16[8,1024]{1,0:T(8,128)(2,1)S(1)} %copy.12), channel_id=1, source_target_pairs={{240,0},{0,16},{16,32},{32,48},{48,64},{64,80},{80,96},{96,112},{1... | collective-permute-start | bytes 49160 | tf_op jit(solution)/shard_map/while/body/eval_jaxpr/ppermute | solution.py:12
  358.9 7.6 collective-permute-start.1
  366.5 80.3 %reduce-scatter.2.cloned.1.call-start = ((), (), s32[]{:S(2)}) async-start(), calls=%async_computation.1 | async-start | bytes 557056 | tf_op jit(solution)/shard_map/while/body/eval_jaxpr/reduce_scatter | solution.py:39
  389.6 65.5 %collective-permute-start = (bf16[8,1024]{1,0:T(8,128)(2,1)S(1)}, bf16[8,1024]{1,0:T(8,128)(2,1)S(1)}, u32[]{:S(2)}, u32[]{:S(2)}) collective-permute-start(bf16[8,1024]{1,0:T(8,128)(2,1)S(1)} %copy.12), channel_id=1, source_target_pairs={{240,0},{0,16},{16,32},{32,48},{48,64},{64,80},{80,96},{96,112},{1... | collective-permute-start | bytes 49160 | tf_op jit(solution)/shard_map/while/body/eval_jaxpr/ppermute | solution.py:12
  447.5 7.6 collective-permute-start.1
  455.1 80.3 %reduce-scatter.2.cloned.1.call-start = ((), (), s32[]{:S(2)}) async-start(), calls=%async_computation.1 | async-start | bytes 557056 | tf_op jit(solution)/shard_map/while/body/eval_jaxpr/reduce_scatter | solution.py:39
  478.3 65.5 %collective-permute-start = (bf16[8,1024]{1,0:T(8,128)(2,1)S(1)}, bf16[8,1024]{1,0:T(8,128)(2,1)S(1)}, u32[]{:S(2)}, u32[]{:S(2)}) collective-permute-start(bf16[8,1024]{1,0:T(8,128)(2,1)S(1)} %copy.12), channel_id=1, source_target_pairs={{240,0},{0,16},{16,32},{32,48},{48,64},{64,80},{80,96},{96,112},{1... | collective-permute-start | bytes 49160 | tf_op jit(solution)/shard_map/while/body/eval_jaxpr/ppermute | solution.py:12
  536.2 7.6 collective-permute-start.1
  543.8 80.3 %reduce-scatter.2.cloned.1.call-start = ((), (), s32[]{:S(2)}) async-start(), calls=%async_computation.1 | async-start | bytes 557056 | tf_op jit(solution)/shard_map/while/body/eval_jaxpr/reduce_scatter | solution.py:39
  567.0 65.5 %collective-permute-start = (bf16[8,1024]{1,0:T(8,128)(2,1)S(1)}, bf16[8,1024]{1,0:T(8,128)(2,1)S(1)}, u32[]{:S(2)}, u32[]{:S(2)}) collective-permute-start(bf16[8,1024]{1,0:T(8,128)(2,1)S(1)} %copy.12), channel_id=1, source_target_pairs={{240,0},{0,16},{16,32},{32,48},{48,64},{64,80},{80,96},{96,112},{1... | collective-permute-start | bytes 49160 | tf_op jit(solution)/shard_map/while/body/eval_jaxpr/ppermute | solution.py:12
  624.9 7.6 collective-permute-start.1
  632.5 80.3 %reduce-scatter.2.cloned.1.call-start = ((), (), s32[]{:S(2)}) async-start(), calls=%async_computation.1 | async-start | bytes 557056 | tf_op jit(solution)/shard_map/while/body/eval_jaxpr/reduce_scatter | solution.py:39
  655.6 65.5 %collective-permute-start = (bf16[8,1024]{1,0:T(8,128)(2,1)S(1)}, bf16[8,1024]{1,0:T(8,128)(2,1)S(1)}, u32[]{:S(2)}, u32[]{:S(2)}) collective-permute-start(bf16[8,1024]{1,0:T(8,128)(2,1)S(1)} %copy.12), channel_id=1, source_target_pairs={{240,0},{0,16},{16,32},{32,48},{48,64},{64,80},{80,96},{96,112},{1... | collective-permute-start | bytes 49160 | tf_op jit(solution)/shard_map/while/body/eval_jaxpr/ppermute | solution.py:12
  713.5 7.6 collective-permute-start.1
  721.1 80.3 %reduce-scatter.2.cloned.1.call-start = ((), (), s32[]{:S(2)}) async-start(), calls=%async_computation.1 | async-start | bytes 557056 | tf_op jit(solution)/shard_map/while/body/eval_jaxpr/reduce_scatter | solution.py:39
  744.3 65.5 %collective-permute-start = (bf16[8,1024]{1,0:T(8,128)(2,1)S(1)}, bf16[8,1024]{1,0:T(8,128)(2,1)S(1)}, u32[]{:S(2)}, u32[]{:S(2)}) collective-permute-start(bf16[8,1024]{1,0:T(8,128)(2,1)S(1)} %copy.12), channel_id=1, source_target_pairs={{240,0},{0,16},{16,32},{32,48},{48,64},{64,80},{80,96},{96,112},{1... | collective-permute-start | bytes 49160 | tf_op jit(solution)/shard_map/while/body/eval_jaxpr/ppermute | solution.py:12
  802.2 7.6 collective-permute-start.1
  809.8 80.3 %reduce-scatter.2.cloned.1.call-start = ((), (), s32[]{:S(2)}) async-start(), calls=%async_computation.1 | async-start | bytes 557056 | tf_op jit(solution)/shard_map/while/body/eval_jaxpr/reduce_scatter | solution.py:39
  833.0 65.5 %collective-permute-start = (bf16[8,1024]{1,0:T(8,128)(2,1)S(1)}, bf16[8,1024]{1,0:T(8,128)(2,1)S(1)}, u32[]{:S(2)}, u32[]{:S(2)}) collective-permute-start(bf16[8,1024]{1,0:T(8,128)(2,1)S(1)} %copy.12), channel_id=1, source_target_pairs={{240,0},{0,16},{16,32},{32,48},{48,64},{64,80},{80,96},{96,112},{1... | collective-permute-start | bytes 49160 | tf_op jit(solution)/shard_map/while/body/eval_jaxpr/ppermute | solution.py:12
  890.9 7.6 collective-permute-start.1
  898.5 80.3 %reduce-scatter.2.cloned.1.call-start = ((), (), s32[]{:S(2)}) async-start(), calls=%async_computation.1 | async-start | bytes 557056 | tf_op jit(solution)/shard_map/while/body/eval_jaxpr/reduce_scatter | solution.py:39
  921.7 65.5 %collective-permute-start = (bf16[8,1024]{1,0:T(8,128)(2,1)S(1)}, bf16[8,1024]{1,0:T(8,128)(2,1)S(1)}, u32[]{:S(2)}, u32[]{:S(2)}) collective-permute-start(bf16[8,1024]{1,0:T(8,128)(2,1)S(1)} %copy.12), channel_id=1, source_target_pairs={{240,0},{0,16},{16,32},{32,48},{48,64},{64,80},{80,96},{96,112},{1... | collective-permute-start | bytes 49160 | tf_op jit(solution)/shard_map/while/body/eval_jaxpr/ppermute | solution.py:12
  979.6 7.6 collective-permute-start.1
  987.1 80.4 %reduce-scatter.2.cloned.1.call-start = ((), (), s32[]{:S(2)}) async-start(), calls=%async_computation.1 | async-start | bytes 557056 | tf_op jit(solution)/shard_map/while/body/eval_jaxpr/reduce_scatter | solution.py:39
  1010.3 65.5 %collective-permute-start = (bf16[8,1024]{1,0:T(8,128)(2,1)S(1)}, bf16[8,1024]{1,0:T(8,128)(2,1)S(1)}, u32[]{:S(2)}, u32[]{:S(2)}) collective-permute-start(bf16[8,1024]{1,0:T(8,128)(2,1)S(1)} %copy.12), channel_id=1, source_target_pairs={{240,0},{0,16},{16,32},{32,48},{48,64},{64,80},{80,96},{96,112},{1... | collective-permute-start | bytes 49160 | tf_op jit(solution)/shard_map/while/body/eval_jaxpr/ppermute | solution.py:12
  1068.3 7.6 collective-permute-start.1
  1075.8 80.3 %reduce-scatter.2.cloned.1.call-start = ((), (), s32[]{:S(2)}) async-start(), calls=%async_computation.1 | async-start | bytes 557056 | tf_op jit(solution)/shard_map/while/body/eval_jaxpr/reduce_scatter | solution.py:39
  1099.0 65.5 %collective-permute-start = (bf16[8,1024]{1,0:T(8,128)(2,1)S(1)}, bf16[8,1024]{1,0:T(8,128)(2,1)S(1)}, u32[]{:S(2)}, u32[]{:S(2)}) collective-permute-start(bf16[8,1024]{1,0:T(8,128)(2,1)S(1)} %copy.12), channel_id=1, source_target_pairs={{240,0},{0,16},{16,32},{32,48},{48,64},{64,80},{80,96},{96,112},{1... | collective-permute-start | bytes 49160 | tf_op jit(solution)/shard_map/while/body/eval_jaxpr/ppermute | solution.py:12
  1156.9 7.6 collective-permute-start.1
  1164.6 80.3 %reduce-scatter.2.cloned.1.call-start = ((), (), s32[]{:S(2)}) async-start(), calls=%async_computation.1 | async-start | bytes 557056 | tf_op jit(solution)/shard_map/while/body/eval_jaxpr/reduce_scatter | solution.py:39
  1187.7 65.5 %collective-permute-start = (bf16[8,1024]{1,0:T(8,128)(2,1)S(1)}, bf16[8,1024]{1,0:T(8,128)(2,1)S(1)}, u32[]{:S(2)}, u32[]{:S(2)}) collective-permute-start(bf16[8,1024]{1,0:T(8,128)(2,1)S(1)} %copy.12), channel_id=1, source_target_pairs={{240,0},{0,16},{16,32},{32,48},{48,64},{64,80},{80,96},{96,112},{1... | collective-permute-start | bytes 49160 | tf_op jit(solution)/shard_map/while/body/eval_jaxpr/ppermute | solution.py:12
  1245.6 7.5 collective-permute-start.1
  1253.2 80.3 %reduce-scatter.2.cloned.1.call-start = ((), (), s32[]{:S(2)}) async-start(), calls=%async_computation.1 | async-start | bytes 557056 | tf_op jit(solution)/shard_map/while/body/eval_jaxpr/reduce_scatter | solution.py:39
  1276.3 65.6 %collective-permute-start = (bf16[8,1024]{1,0:T(8,128)(2,1)S(1)}, bf16[8,1024]{1,0:T(8,128)(2,1)S(1)}, u32[]{:S(2)}, u32[]{:S(2)}) collective-permute-start(bf16[8,1024]{1,0:T(8,128)(2,1)S(1)} %copy.12), channel_id=1, source_target_pairs={{240,0},{0,16},{16,32},{32,48},{48,64},{64,80},{80,96},{96,112},{1... | collective-permute-start | bytes 49160 | tf_op jit(solution)/shard_map/while/body/eval_jaxpr/ppermute | solution.py:12
  1334.3 7.6 collective-permute-start.1
  1341.9 80.3 %reduce-scatter.2.cloned.1.call-start = ((), (), s32[]{:S(2)}) async-start(), calls=%async_computation.1 | async-start | bytes 557056 | tf_op jit(solution)/shard_map/while/body/eval_jaxpr/reduce_scatter | solution.py:39
  1365.0 65.5 %collective-permute-start = (bf16[8,1024]{1,0:T(8,128)(2,1)S(1)}, bf16[8,1024]{1,0:T(8,128)(2,1)S(1)}, u32[]{:S(2)}, u32[]{:S(2)}) collective-permute-start(bf16[8,1024]{1,0:T(8,128)(2,1)S(1)} %copy.12), channel_id=1, source_target_pairs={{240,0},{0,16},{16,32},{32,48},{48,64},{64,80},{80,96},{96,112},{1... | collective-permute-start | bytes 49160 | tf_op jit(solution)/shard_map/while/body/eval_jaxpr/ppermute | solution.py:12
  1422.9 7.6 collective-permute-start.1
Sparse Core Ops, SparseCore 0:
  31.6 60.9 reduce-scatter.1
  124.1 56.6 reduce-scatter.1
  212.4 56.9 reduce-scatter.1
  301.1 56.9 reduce-scatter.1
  389.8 56.9 reduce-scatter.1
  478.4 56.9 reduce-scatter.1
  567.1 56.9 reduce-scatter.1
  655.8 56.9 reduce-scatter.1
  744.4 56.9 reduce-scatter.1
  833.1 56.9 reduce-scatter.1
  921.8 56.9 reduce-scatter.1
  1010.5 56.9 reduce-scatter.1
  1099.1 56.9 reduce-scatter.1
  1187.8 56.9 reduce-scatter.1
  1276.5 56.9 reduce-scatter.1
  1365.2 56.9 reduce-scatter.1
where the time goes:
time: 1440 us
  waiting for transfers between devices  891 us (62%)
  blocking collectives  335 us (23%)
  matrix products  108 us (8%)
  starting transfers between devices  72.5 us (5%)
  other arithmetic  15.5 us (1%)
    reduce_scatter x16, waiting for transfers between devices, turn(): lax.psum_scatter(logit_scale * jnp.einsum('rt,rd->td', coeffs, image_low,...  889 us
    all_gather x16, blocking collectives, turn(): lax.all_gather(shard.astype(jnp.bfloat16), 'group', axis=0, tiled=True)  335 us
    dot_general x16, matrix products, tile(): jnp.dot(coeffs, panel, preferred_element_type=jnp.float32)  76.2 us
    ppermute x32, starting transfers between devices, shifted(): return lax.ppermute(block, axis, route)  72 us
  transfers between devices with their start and end apart: 48, of which 17 were waited for; matrix products, arithmetic and copies ran while one was open for 6% of the time, Pallas kernels for 0%

commit v1 on v0

v1 whole, which is shorter than its diff:
```python
import jax
import jax.numpy as jnp
from jax import lax
from jax.sharding import PartitionSpec as P

logit_scale = 100.0


def shards(images, texts, row_lse, row_weights, pair_ids):
    image_low = images.astype(jnp.bfloat16)
    panel = lax.all_gather(texts.astype(jnp.bfloat16), ("blk", "group"), axis=0, tiled=True)
    columns = jnp.arange(panel.shape[0], dtype=jnp.int32)
    scores = jnp.einsum("rd,td->rt", image_low, panel, preferred_element_type=jnp.float32)
    match = (pair_ids[:, None] == columns[None, :]).astype(jnp.float32)
    coeffs = row_weights[:, None] * (jnp.exp(logit_scale * scores - row_lse[:, None]) - match)
    coeffs = coeffs.astype(jnp.bfloat16)
    terms = jnp.einsum("rt,rd->td", coeffs, image_low, preferred_element_type=jnp.float32)
    reduced = lax.psum_scatter(terms, ("blk", "group"), scatter_dimension=0, tiled=True)
    grads = logit_scale * jnp.dot(coeffs, panel, preferred_element_type=jnp.float32)
    return (grads, logit_scale * reduced)


def solution(mesh):
    placed = (
        P(("blk", "group"), None),
        P(("blk", "group"), None),
        P(("blk", "group")),
        P(("blk", "group")),
        P(("blk", "group")),
    )
    return jax.shard_map(
        shards,
        mesh=mesh,
        in_specs=placed,
        out_specs=(P(("blk", "group"), None), P(("blk", "group"), None)),
        check_vma=False,
    )
```

time: 1440 us -> 1440 us (level)
  waiting for transfers between devices: 891 us -> 1390 us
  blocking collectives: 335 us -> 0 us
  matrix products: 108 us -> 26.2 us
  starting transfers between devices: 72.5 us -> 0.08 us
    reduce_scatter x16 -> x1, waiting for transfers between devices: 889 us -> 1260 us  [shards(): lax.psum_scatter(terms, ('blk', 'group'), scatter_dimension=0, tiled=True)]
    all_gather x16 -> x0, blocking collectives: 335 us -> none  [turn(): lax.all_gather(shard.astype(jnp.bfloat16), 'group', axis=0, tiled=True)]
    all_gather x0 -> x1, waiting for transfers between devices: none -> 122 us  [shards(): lax.all_gather(texts.astype(jnp.bfloat16), ('blk', 'group'), axis=0, tile...]
    dot_general x48 -> x3, matrix products: 108 us -> 26.2 us  [the longest x1 9.97 us: shards(): jnp.dot(coeffs, panel, preferred_element_type=jnp.float32)]
    ppermute x32 -> x0, starting transfers between devices: 72 us -> none  [shifted(): return lax.ppermute(block, axis, route)]
  transfers between devices with their start and end apart: 48 -> 2, of which waited for: 17 -> 2; matrix products, arithmetic and copies ran while one was open for 6% -> 1% of each run, Pallas kernels for 0% -> 0%
where the time goes in v1:
time: 1440 us; the launch traced here: 1430 us
  waiting for transfers between devices  1390 us (97%)
  matrix products  26.2 us (2%)
    reduce_scatter x1, waiting for transfers between devices, shards(): lax.psum_scatter(terms, ('blk', 'group'), scatter_dimension=0, tiled=True)  1260 us
    all_gather x1, waiting for transfers between devices, shards(): lax.all_gather(texts.astype(jnp.bfloat16), ('blk', 'group'), axis=0, tile...  122 us
  transfers between devices with their start and end apart: 2, of which 2 were waited for; matrix products, arithmetic and copies ran while one was open for 1% of the time, Pallas kernels for 0%

profile of v1, /device:TPU:8, one launch (start us, length us, event | category | flops | bytes accessed | tf_op | source)
XLA Modules:
  0.0 1431.1 jit_solution(4617955435436534699)
XLA Ops:
  7.2 0.0 all-gather.2.cloned.1.call-start
  7.2 1.4 convert_element_type.13
  8.6 0.0 all-gather.2.cloned.1.call-update
  8.6 0.0 reduce-scatter.2.cloned.1.call-start
  8.7 121.6 %all-gather.2.cloned.1.call-done = bf16[2048,1024]{1,0:T(8,128)(2,1)} async-done(((bf16[8,1024]{1,0:T(8,128)(2,1)}), bf16[2048,1024]{1,0:T(8,128)(2,1)}) %all-gather.2.cloned.1.call-update) | async-done | bytes 4194320 | tf_op jit(solution)/shard_map/all_gather | solution.py:11
  130.2 0.0 copy-start
  130.2 9.2 multiply_convert_fusion
  139.4 0.0 copy-start.1
  139.4 1.9 copy-done.1
  141.4 0.0 copy-done
  141.4 7.0 fusion
  148.4 0.0 reduce-scatter.2.cloned.1.call-update
  148.4 10.0 convolution_multiply_fusion
  158.4 1264.5 %reduce-scatter.2.cloned.1.call-done = f32[8,1024]{1,0:T(8,128)} async-done(((f32[2048,1024]{1,0:T(8,128)}), f32[8,1024]{1,0:T(8,128)}) %reduce-scatter.2.cloned.1.call-update) | async-done | bytes 32784 | tf_op jit(solution)/shard_map/reduce_scatter | solution.py:18
  1422.9 1.4 broadcast_multiply_fusion
Async XLA Ops:
  7.2 123.0 %all-gather.2.cloned.1.call-start = ((), (), s32[]{:S(2)}) async-start(), calls=%async_computation.1 | async-start | bytes 4210688 | tf_op jit(solution)/shard_map/all_gather | solution.py:11
  8.6 1414.3 %reduce-scatter.2.cloned.1.call-start = ((), (), s32[]{:S(2)}) async-start(), calls=%async_computation.2 | async-start | bytes 8421376 | tf_op jit(solution)/shard_map/reduce_scatter | solution.py:18
  130.2 11.2 copy-start
  139.4 1.9 copy-start.1
Sparse Core Ops, SparseCore 0:
  12.3 117.8 all-gather.1
  148.6 1274.3 reduce-scatter.1

commit v2 on v1

v2 whole, which is shorter than its diff:
```python
import math

import jax
import jax.numpy as jnp
from jax import lax
from jax.experimental import pallas as pl
from jax.experimental.pallas import tpu as pltpu
from jax.sharding import PartitionSpec as P

logit_scale = 100.0
log2e = math.log2(math.e)

MESH = pl.DeviceIdType.MESH
BF, F32 = jnp.bfloat16, jnp.float32
NN = (((1,), (0,)), ((), ()))
NT = (((1,), (1,)), ((), ()))
TN = (((0,), (0,)), ((), ()))

NX, NY, NZ = 4, 4, 8
ROWS, D = 1024, 1024
TEXTS = 1024
GROUP = 256
HALF = D // 2


def device(x, y, z, c):
    return (z * 2 + x // 2, (x % 2) * 8 + y * 2 + c)


def dot(a, b, dims):
    return lax.dot_general(a, b, dims, preferred_element_type=F32)


def kernel(
    images, texts, lse, weights, ids, out_images, out_texts,
    stage, held, vec, blobs, panel, coeffs, own, sent, got, summed, got1, zsum, got2, igs, igr, outs,
    in_sem, out_sem, core_s, core_r, vec_s, vec_r, z_s, z_r, a_s, a_r, b_s, b_r, d_s, d_r,
    e_s, e_r, f_s, f_r, g_s, g_r, h_s, h_r,
):
    blk, group = lax.axis_index("blk"), lax.axis_index("group")
    z, x = blk // 2, (blk % 2) * 2 + group // 8
    y, c = (group // 2) % 4, group % 2
    last, first = (x, y), (y, x)

    def on_last(h, o):
        return device((x + o) % NX, y, z, c) if h == 0 else device(x, (y + o) % NY, z, c)

    def on_first(h, o):
        return on_last(1 - h, o)

    def on_z(o):
        return device(x, y, (z + o) % NZ, c)

    partner = device(x, y, z, 1 - c)

    barrier = pltpu.get_barrier_semaphore()
    peers = [partner] + [on_z(o) for o in range(1, NZ)]
    peers += [on_last(h, o) for h in range(2) for o in range(1, 4)]
    for peer in peers:
        pl.semaphore_signal(barrier, inc=1, device_id=peer, device_id_type=MESH)

    loads = []
    for k in range(4):
        rows = pl.ds(k * 256, 256)
        load = pltpu.make_async_copy(images.at[rows], stage.at[rows], in_sem.at[k])
        load.start()
        loads.append(load)

    sends = []

    def send(src, dst, ss, rs, peer):
        copy = pltpu.make_async_remote_copy(
            src_ref=src, dst_ref=dst, send_sem=ss, recv_sem=rs, device_id=peer, device_id_type=MESH
        )
        copy.start()
        sends.append(copy)
        return copy

    zh = z // 4
    za = x * (1 - zh) + y * zh
    zb = y * (1 - zh) + x * zh
    place = blobs.at[zh, za, zb, pl.ds(pl.multiple_of((z % 4) * 16, 16), 16)]
    t = texts[...]
    place[...] = jnp.concatenate([t[:, :HALF], t[:, HALF:]], axis=0).astype(BF)

    pl.semaphore_wait(barrier, len(peers))

    z_copies = [send(place, place, z_s.at[o - 1], z_r.at[o - 1], on_z(o)) for o in (1, 7, 2, 6, 3, 5, 4)]

    vec[0] = jnp.zeros((8, ROWS), F32)
    w = weights[...]
    vec[0, 0:1] = (jnp.log(w) - lse[...]) * log2e
    vec[0, 1:2] = ids[...].astype(F32)
    vec[0, 2:3] = w
    vec_copy = send(vec.at[0], vec.at[1], vec_s, vec_r, partner)

    core_copies = []
    for k in range(4):
        rows = pl.ds(k * 256, 256)
        loads[k].wait()
        held[rows] = stage[rows].astype(BF)
        core_copies.append(
            send(held.at[rows], held.at[pl.ds(ROWS + k * 256, 256)], core_s.at[k], core_r.at[k], partner)
        )

    for copy in z_copies:
        copy.wait_recv()

    a_copies = [[None] * 4 for _ in range(2)]
    b_copies = [[[None] * 4 for _ in range(2)] for _ in range(2)]

    def to_last(h, o):
        f = (first[h] - o + 4) % 4
        blob = blobs.at[h, last[h], f]
        for way, step in ((0, 1), (1, 3)):
            b_copies[h][way][o] = send(blob, blob, b_s.at[h, way, o], b_r.at[h, way, f], on_last(h, step))

    for h in range(2):
        blob = blobs.at[h, last[h], first[h]]
        for o in (1, 3, 2):
            a_copies[h][o] = send(blob, blob, a_s.at[h, o], a_r.at[h, o], on_first(h, o))
    for h in range(2):
        to_last(h, 0)
    for o in (1, 3, 2):
        for h in range(2):
            a_copies[h][o].wait_recv()
            to_last(h, o)

    def unpack(step, g):
        for h in range(2):
            a = (last[h] + step) % 4
            blob = blobs[h, a].reshape(GROUP, HALF).astype(F32).reshape(16, 2, 8, HALF)
            rows = pl.ds(g * GROUP + h * 128, 128)
            panel[rows, :HALF] = blob[:, 0].reshape(128, HALF).astype(BF)
            panel[rows, HALF:] = blob[:, 1].reshape(128, HALF).astype(BF)

    def scores(step, g):
        rows = pl.ds(g * GROUP, GROUP)
        r = lax.broadcasted_iota(jnp.int32, (GROUP, 1), 0)
        upper = r >= 128
        b = (r & 127) >> 5
        zz = ((r >> 7) << 2) + ((r & 31) >> 3)
        tx = jnp.where(upper, b, (x + step) % 4)
        ty = jnp.where(upper, (y + step) % 4, b)
        number = (zz * 256 + tx * 64 + ty * 16 + c * 8 + (r & 7)).astype(F32)

        for side in range(2):
            for k in range(4):
                lanes = slice(k * 256, (k + 1) * 256)
                cols = slice(side * ROWS + k * 256, side * ROWS + (k + 1) * 256)
                s = dot(panel[rows], held[cols], NT)
                e = jnp.exp2(s * (logit_scale * log2e) + vec[side, 0:1, lanes])
                e = e - jnp.where(number == vec[side, 1:2, lanes], vec[side, 2:3, lanes], 0.0)
                coeffs[rows, cols] = e.astype(BF)

    def terms(g, keep):
        rows = pl.ds(g * GROUP, GROUP)
        for j in range(2):
            lo = dot(coeffs[rows], held[:, j * 256 : (j + 1) * 256], NN)
            hi = dot(coeffs[rows], held[:, HALF + j * 256 : HALF + (j + 1) * 256], NN)
            both = jnp.stack([lo.reshape(32, 8, 256), hi.reshape(32, 8, 256)], axis=1).reshape(512, 256)
            keep(j, both)

    def keep_own(j, both):
        own[:, j * 256 : (j + 1) * 256] = both

    def keep_sent(g):
        def keep(j, both):
            sent[g - 1, :, j * 256 : (j + 1) * 256] = both.astype(BF)

        return keep

    for copy in core_copies:
        copy.wait_recv()
    vec_copy.wait_recv()

    unpack(0, 0)
    scores(0, 0)

    d_copies = [[None] * 4 for _ in range(2)]

    def arrived(h, way, f):
        a = (last[h] + (3 if way == 0 else 1)) % 4
        blob = blobs.at[h, a, f]
        return pltpu.make_async_remote_copy(
            src_ref=blob, dst_ref=blob, send_sem=b_s.at[h, way, 0], recv_sem=b_r.at[h, way, f],
            device_id=on_last(h, 1), device_id_type=MESH,
        ), blob

    for f in range(4):
        for h in range(2):
            way = 0 if f < 2 else 1
            copy, blob = arrived(h, way, f)
            copy.wait_recv()
            d_copies[h][f] = send(blob, blob, d_s.at[h, f], d_r.at[h, f], on_last(h, 1 if way == 0 else 3))
    for f in range(4):
        for h in range(2):
            copy, _ = arrived(h, 1 if f < 2 else 0, f)
            copy.wait_recv()

    e_copies = [[None] * 2 for _ in range(4)]
    for g, step in ((1, 3), (2, 1), (3, 2)):
        if g == 3:
            for h in range(2):
                for f in range(4):
                    d_copies[h][f].wait_recv()
        unpack(step, g)
        scores(step, g)
        terms(g, keep_sent(g))
        for h in range(2):
            half = pl.ds(h * 256, 256)
            e_copies[g][h] = send(
                sent.at[g - 1, half], got.at[g - 1, half], e_s.at[g - 1, h], e_r.at[g - 1, h], on_last(h, step)
            )
    terms(0, keep_own)

    f_copies = []

    def image_rows(k, base, keep):
        cols = slice(base + k * 256, base + (k + 1) * 256)
        for j in range(4):
            lanes = slice(j * 256, (j + 1) * 256)
            keep(k, lanes, dot(coeffs[:, cols], panel[:, lanes], TN))

    def keep_partner(k, lanes, grads):
        igs[k * 256 : (k + 1) * 256, lanes] = grads.astype(BF)

    def keep_mine(k, lanes, grads):
        rows = slice(k * 256, (k + 1) * 256)
        outs[rows, lanes] = (grads + igr[rows, lanes].astype(F32)).astype(BF)

    for k in range(4):
        image_rows(k, ROWS, keep_partner)
        rows = pl.ds(k * 256, 256)
        f_copies.append(send(igs.at[rows], igr.at[rows], f_s.at[k], f_r.at[k], partner))
    stores = []
    for k in range(4):
        rows = pl.ds(k * 256, 256)
        f_copies[k].wait_recv()
        image_rows(k, 0, keep_mine)
        store = pltpu.make_async_copy(outs.at[rows], out_images.at[rows], out_sem.at[k])
        store.start()
        stores.append(store)

    g_copies = []
    for h in range(2):
        half = pl.ds(h * 256, 256)
        total = own[half]
        for g in range(3):
            e_copies[g + 1][h].wait_recv()
            total = total + got[g, half].astype(F32)
        summed[half] = total.astype(BF)
        for o in (1, 3, 2):
            f = (first[h] + o) % 4
            rows = pl.ds(pl.multiple_of(h * 256 + f * 64, 64), 64)
            there = got1.at[o - 1, pl.ds(h * 64, 64)]
            g_copies.append(send(summed.at[rows], there, g_s.at[h, o - 1], g_r.at[h, o - 1], on_first(h, o)))
    for copy in g_copies:
        copy.wait_recv()
    for h in range(2):
        mine = summed[pl.ds(pl.multiple_of(h * 256 + first[h] * 64, 64), 64)].astype(F32)
        rows = pl.ds(h * 64, 64)
        for o in range(3):
            mine = mine + got1[o, rows].astype(F32)
        zsum[rows] = mine.astype(BF)
    h_copies = []
    for o in (1, 7, 2, 6, 3, 5, 4):
        rows = pl.ds(pl.multiple_of(((z + o) % NZ) * 16, 16), 16)
        h_copies.append(send(zsum.at[rows], got2.at[o - 1], h_s.at[o - 1], h_r.at[o - 1], on_z(o)))
    total = zsum[pl.ds(pl.multiple_of(z * 16, 16), 16)].astype(F32)
    for copy in h_copies:
        copy.wait_recv()
    for o in range(7):
        total = total + got2[o].astype(F32)
    total = total * logit_scale
    out_texts[:, :HALF] = total[:8]
    out_texts[:, HALF:] = total[8:]

    for copy in sends:
        copy.wait_send()
    for store in stores:
        store.wait()


def shards(images, texts, row_lse, row_weights, pair_ids):
    vm = pl.BlockSpec(memory_space=pltpu.VMEM)
    hbm = pl.BlockSpec(memory_space=pl.ANY)
    dma = pltpu.SemaphoreType.DMA
    grads, text_grads = pl.pallas_call(
        kernel,
        out_shape=(
            jax.ShapeDtypeStruct((ROWS, D), BF),
            jax.ShapeDtypeStruct((8, D), F32),
        ),
        in_specs=[hbm, vm, vm, vm, vm],
        out_specs=(hbm, vm),
        scratch_shapes=[
            pltpu.VMEM((ROWS, D), F32),
            pltpu.VMEM((2 * ROWS, D), BF),
            pltpu.VMEM((2, 8, ROWS), F32),
            pltpu.VMEM((2, 4, 4, 64, HALF), BF),
            pltpu.VMEM((TEXTS, D), BF),
            pltpu.VMEM((TEXTS, 2 * ROWS), BF),
            pltpu.VMEM((512, HALF), F32),
            pltpu.VMEM((3, 512, HALF), BF),
            pltpu.VMEM((3, 512, HALF), BF),
            pltpu.VMEM((512, HALF), BF),
            pltpu.VMEM((3, 128, HALF), BF),
            pltpu.VMEM((128, HALF), BF),
            pltpu.VMEM((7, 16, HALF), BF),
            pltpu.VMEM((ROWS, D), BF),
            pltpu.VMEM((ROWS, D), BF),
            pltpu.VMEM((ROWS, D), BF),
            dma((4,)), dma((4,)), dma((4,)), dma((4,)), dma, dma, dma((7,)), dma((7,)),
            dma((2, 4)), dma((2, 4)), dma((2, 2, 4)), dma((2, 2, 4)), dma((2, 4)), dma((2, 4)),
            dma((3, 2)), dma((3, 2)), dma((4,)), dma((4,)), dma((2, 3)), dma((2, 3)), dma((7,)), dma((7,)),
        ],
        compiler_params=pltpu.CompilerParams(
            collective_id=0, has_side_effects=True, vmem_limit_bytes=48 << 20
        ),
        name="tile",
    )(
        images, texts, row_lse.reshape(1, ROWS), row_weights.reshape(1, ROWS), pair_ids.reshape(1, ROWS)
    )
    return logit_scale * grads.astype(F32), text_grads


def solution(mesh):
    placed = (
        P(("blk", "group"), None),
        P(("blk", "group"), None),
        P(("blk", "group")),
        P(("blk", "group")),
        P(("blk", "group")),
    )
    return jax.shard_map(
        shards,
        mesh=mesh,
        in_specs=placed,
        out_specs=(P(("blk", "group"), None), P(("blk", "group"), None)),
        check_vma=False,
    )
```

time: 1440 us -> 61.4 us (0.04)
  waiting for transfers between devices: 1390 us -> 0 us
  Pallas kernels: 0 us -> 54 us
  matrix products: 26.2 us -> 0 us
    reduce_scatter x1 -> x0, waiting for transfers between devices: 1260 us -> none  [shards(): lax.psum_scatter(terms, ('blk', 'group'), scatter_dimension=0, tiled=True)]
    all_gather x1 -> x0, waiting for transfers between devices: 122 us -> none  [shards(): lax.all_gather(texts.astype(jnp.bfloat16), ('blk', 'group'), axis=0, tile...]
    pallas_call x0 -> x1, Pallas kernels: none -> 54 us  [shards(): pl.pallas_call(kernel, out_shape=(jax.ShapeDtypeStruct((ROWS, D), BF), ja...]
    dot_general x3 -> x0, matrix products: 26.2 us -> none  [the longest x1 9.97 us: shards(): jnp.dot(coeffs, panel, preferred_element_type=jnp.float32)]
  transfers between devices with their start and end apart: 2 -> 0, of which waited for: 2 -> 0; matrix products, arithmetic and copies ran while one was open for 1% -> 0% of each run, Pallas kernels for 0% -> 0%
where the time goes in v2:
time: 61.4 us; the launch traced here: 60.7 us
  Pallas kernels  54 us (88%)
  local copies, waits for them, and re-layouts  3.42 us (6%)
  other arithmetic  2.58 us (4%)
  between operations  0.65 us (1%)
    pallas_call x1, Pallas kernels, shards(): pl.pallas_call(kernel, out_shape=(jax.ShapeDtypeStruct((ROWS, D), BF), ja...  54 us
    unnamed x9, local copies, waits for them, and re-layouts  3.42 us
    mul x1, other arithmetic, shards(): return (logit_scale * grads.astype(F32), text_grads)  2.58 us

profile of v2, /device:TPU:8, one launch (start us, length us, event | category | flops | bytes accessed | tf_op | source)
XLA Modules:
  0.0 60.7 jit_solution(8204731960361588297)
XLA Ops:
  0.6 0.0 copy-start
  0.6 0.7 %copy-done = f32[8,1024]{1,0:T(8,128)S(1)} copy-done((f32[8,1024]{1,0:T(8,128)S(1)}, f32[8,1024]{1,0:T(8,128)}, u32[]{:S(2)}) %copy-start) | copy-done | bytes 32792
  1.4 0.0 copy-start.1
  1.4 0.7 %copy-done.1 = f32[1024]{0:T(1024)S(1)} copy-done((f32[1024]{0:T(1024)S(1)}, f32[1024]{0:T(1024)}, u32[]{:S(2)}) %copy-start.1) | copy-done | bytes 4120
  2.1 0.0 copy-start.2
  2.1 0.7 %copy-done.2 = f32[1024]{0:T(1024)S(1)} copy-done((f32[1024]{0:T(1024)S(1)}, f32[1024]{0:T(1024)}, u32[]{:S(2)}) %copy-start.2) | copy-done | bytes 4120
  2.8 0.0 copy-start.3
  2.8 0.7 %copy-done.3 = s32[1024]{0:T(1024)S(1)} copy-done((s32[1024]{0:T(1024)S(1)}, s32[1024]{0:T(1024)}, u32[]{:S(2)}) %copy-start.3) | copy-done | bytes 4120
  3.5 54.0 %tile.1 = (bf16[1024,1024]{1,0:T(8,128)(2,1)S(1)}, f32[8,1024]{1,0:T(8,128)S(1)}) custom-call(f32[1024,1024]{1,0:T(8,128)} %images.1, f32[8,1024]{1,0:T(8,128)S(1)} %copy-done, f32[1,1024]{1,0:T(1,128)S(1)} %bitcast.3, f32[1,1024]{1,0:T(1,128)S(1)} %bitcast.4, s32[1,1024]{1,0:T(1,128)S(1)} %bitcast.5), custom_call_target="tpu_custom_call" | custom-call | tf_op jit(solution)/shard_map/tile/pallas_call | solution.py:289
  57.5 2.6 %convert_multiply_fusion = f32[1024,1024]{1,0:T(8,128)} fusion(bf16[1024,1024]{1,0:T(8,128)(2,1)S(1)} %get-tuple-element.4), kind=kLoop, calls=%fused_computation | loop fusion | flops 2097152 | bytes 6291456 | tf_op jit(solution)/shard_map/mul | solution.py:325
  60.1 0.6 %copy.8 = f32[8,1024]{1,0:T(8,128)} copy(f32[8,1024]{1,0:T(8,128)S(1)} %get-tuple-element.9) | data formatting | bytes 65536
Async XLA Ops:
  0.6 0.8 %copy-start = (f32[8,1024]{1,0:T(8,128)S(1)}, f32[8,1024]{1,0:T(8,128)}, u32[]{:S(2)}) copy-start(f32[8,1024]{1,0:T(8,128)} %texts.1) | copy-start | bytes 98308
  1.4 0.7 %copy-start.1 = (f32[1024]{0:T(1024)S(1)}, f32[1024]{0:T(1024)}, u32[]{:S(2)}) copy-start(f32[1024]{0:T(1024)} %param.7) | copy-start | bytes 12292
  2.1 0.7 %copy-start.2 = (f32[1024]{0:T(1024)S(1)}, f32[1024]{0:T(1024)}, u32[]{:S(2)}) copy-start(f32[1024]{0:T(1024)} %param.8) | copy-start | bytes 12292
  2.8 0.7 %copy-start.3 = (s32[1024]{0:T(1024)S(1)}, s32[1024]{0:T(1024)}, u32[]{:S(2)}) copy-start(s32[1024]{0:T(1024)} %param.9) | copy-start | bytes 12292

commit v3 on v2

v3 whole, which is shorter than its diff:
```python
import math

import jax
import jax.numpy as jnp
from jax import lax
from jax.experimental import pallas as pl
from jax.experimental.pallas import tpu as pltpu
from jax.sharding import PartitionSpec as P

logit_scale = 100.0
log2e = math.log2(math.e)

MESH = pl.DeviceIdType.MESH
BF, F32 = jnp.bfloat16, jnp.float32
NN = (((1,), (0,)), ((), ()))
NT = (((1,), (1,)), ((), ()))
TN = (((0,), (0,)), ((), ()))

NX, NY, NZ = 4, 4, 8
ROWS, D = 1024, 1024
TEXTS = 1024
GROUP = 256
HALF = D // 2


def device(x, y, z, c):
    return (z * 2 + x // 2, (x % 2) * 8 + y * 2 + c)


def dot(a, b, dims):
    return lax.dot_general(a, b, dims, preferred_element_type=F32)


def kernel(
    images, texts, lse, weights, ids, out_images, out_texts,
    stage, texts_in, rows_in, ids_in, held, vec, blobs, panel, coeffs, sent, got, summed, done, got1, got2, mine, igs, igr,
    in_sem, row_sem, core_s, core_r, vec_s, vec_r, z_s, z_r, a_s, a_r, b_s, b_r, d_s, d_r,
    e_s, e_r, f_s, f_r, g_s, g_r, h_s, h_r,
):
    blk, group = lax.axis_index("blk"), lax.axis_index("group")
    z, x = blk // 2, (blk % 2) * 2 + group // 8
    y, c = (group // 2) % 4, group % 2
    zh = z // 4
    last, first = (x, y), (y, x)

    def on_last(h, o):
        return device((x + o) % NX, y, z, c) if h == 0 else device(x, (y + o) % NY, z, c)

    def on_first(h, o):
        return on_last(1 - h, o)

    def on_own_first(o):
        return device((x + o * zh) % NX, (y + o * (1 - zh)) % NY, z, c)

    def on_z(o):
        return device(x, y, (z + o) % NZ, c)

    partner = device(x, y, z, 1 - c)

    def load(src, dst, sem):
        copy = pltpu.make_async_copy(src, dst, sem)
        copy.start()
        return copy

    texts_load = load(texts, texts_in, row_sem.at[0])
    barrier = pltpu.get_barrier_semaphore()
    peers = [partner] + [on_z(o) for o in range(1, NZ)]
    peers += [on_last(h, o) for h in range(2) for o in range(1, 4)]
    for peer in peers:
        pl.semaphore_signal(barrier, inc=1, device_id=peer, device_id_type=MESH)

    loads = []
    for k in range(4):
        rows = pl.ds(k * 256, 256)
        loads.append(load(images.at[rows], stage.at[rows], in_sem.at[k]))
    row_loads = [
        load(lse, rows_in.at[pl.ds(0, 1)], row_sem.at[1]),
        load(weights, rows_in.at[pl.ds(1, 1)], row_sem.at[2]),
        load(ids, ids_in, row_sem.at[3]),
    ]

    sends = []

    def send(src, dst, ss, rs, peer):
        copy = pltpu.make_async_remote_copy(
            src_ref=src, dst_ref=dst, send_sem=ss, recv_sem=rs, device_id=peer, device_id_type=MESH
        )
        copy.start()
        sends.append(copy)
        return copy

    za = x * (1 - zh) + y * zh
    zb = y * (1 - zh) + x * zh
    place = blobs.at[zh, za, zb, pl.ds(pl.multiple_of((z % 4) * 16, 16), 16)]
    texts_load.wait()
    t = texts_in[...]
    place[...] = jnp.concatenate([t[:, :HALF], t[:, HALF:]], axis=0).astype(BF)

    pl.semaphore_wait(barrier, len(peers))

    z_copies = [send(place, place, z_s.at[o - 1], z_r.at[o - 1], on_z(o)) for o in (1, 7, 2, 6, 3, 5, 4)]

    vec[0] = jnp.zeros((8, ROWS), F32)
    for copy in row_loads:
        copy.wait()
    w = rows_in[1:2]
    vec[0, 0:1] = (jnp.log(w) - rows_in[0:1]) * log2e
    vec[0, 1:2] = ids_in[...].astype(F32)
    vec[0, 2:3] = w
    vec_copy = send(vec.at[0], vec.at[1], vec_s, vec_r, partner)

    for k in range(4):
        rows = pl.ds(k * 256, 256)
        loads[k].wait()
        held[rows] = stage[rows].astype(BF)

    for copy in z_copies:
        copy.wait_recv()

    a_copies, b_copies, d_copies = {}, {}, {}

    def place_of(h, o):
        return (first[h] - o + 4) % 4

    def to_last(h, o):
        blob = blobs.at[h, last[h], place_of(h, o)]
        for way, step in ((0, 1), (1, 3)):
            b_copies[h, way, o] = send(blob, blob, b_s.at[h, way, o], b_r.at[h, way, o], on_last(h, step))
        if o >= 2:
            d_copies[h, o] = send(blob, blob, d_s.at[h, o], d_r.at[h, o], on_last(h, 2))

    def relay(h, o):
        b_copies[h, o, o].wait_recv()
        blob = blobs.at[h, (last[h] + (3 if o == 0 else 1)) % 4, place_of(h, o)]
        d_copies[h, o] = send(blob, blob, d_s.at[h, o], d_r.at[h, o], on_last(h, 1 if o == 0 else 3))

    for h in range(2):
        blob = blobs.at[h, last[h], first[h]]
        for o in (1, 3, 2):
            a_copies[h, o] = send(blob, blob, a_s.at[h, o], a_r.at[h, o], on_first(h, o))
    for h in range(2):
        to_last(h, 0)
    core_copies = []
    for k in range(4):
        rows, there = pl.ds(k * 256, 256), pl.ds(ROWS + k * 256, 256)
        core_copies.append(send(held.at[rows], held.at[there], core_s.at[k], core_r.at[k], partner))
    for o in (1, 3, 2):
        for h in range(2):
            a_copies[h, o].wait_recv()
            to_last(h, o)
        if o == 1:
            for h in range(2):
                relay(h, 0)

    def unpack(o):
        for h in range(2):
            blob = blobs[h, :, place_of(h, o)].reshape(GROUP, HALF).astype(F32).reshape(16, 2, 8, HALF)
            rows = pl.ds(o * GROUP + h * 128, 128)
            panel[rows, :HALF] = blob[:, 0].reshape(128, HALF).astype(BF)
            panel[rows, HALF:] = blob[:, 1].reshape(128, HALF).astype(BF)

    def scores(o):
        rows = pl.ds(o * GROUP, GROUP)
        r = lax.broadcasted_iota(jnp.int32, (GROUP, 1), 0)
        a = (r & 127) >> 5
        zz = ((r >> 7) << 2) + ((r & 31) >> 3)
        chip = jnp.where(r >= 128, place_of(1, o) * 64 + a * 16, place_of(0, o) * 16 + a * 64)
        number = (zz * 256 + chip + c * 8 + (r & 7)).astype(F32)

        for side in range(2):
            for k in range(4):
                lanes = slice(k * 256, (k + 1) * 256)
                cols = slice(side * ROWS + k * 256, side * ROWS + (k + 1) * 256)
                s = dot(panel[rows], held[cols], NT)
                e = jnp.exp2(s * (logit_scale * log2e) + vec[side, 0:1, lanes])
                e = e - jnp.where(number == vec[side, 1:2, lanes], vec[side, 2:3, lanes], 0.0)
                coeffs[rows, cols] = e.astype(BF)

    def terms(o):
        rows = pl.ds(o * GROUP, GROUP)
        for j in range(2):
            lo = dot(coeffs[rows], held[:, j * 256 : (j + 1) * 256], NN)
            hi = dot(coeffs[rows], held[:, HALF + j * 256 : HALF + (j + 1) * 256], NN)
            both = jnp.stack([lo.reshape(32, 8, 256), hi.reshape(32, 8, 256)], axis=1).reshape(512, 256)
            sent[o, :, j * 256 : (j + 1) * 256] = both.astype(BF)

    def block(h, s):
        return pl.ds(pl.multiple_of(h * 256 + ((last[h] + s) % 4) * 64, 64), 64)

    for copy in core_copies:
        copy.wait_recv()
    vec_copy.wait_recv()

    e_copies = {}

    def give_terms(o):
        terms(o)
        for s in (2, 1, 3):
            for h in range(2):
                e_copies[h, o, s] = send(
                    sent.at[o, block(h, s)], got.at[o, h, s - 1],
                    e_s.at[o, h, s - 1], e_r.at[o, h, s - 1], on_last(h, s),
                )

    def over_last(h, o):
        total = sent[o, block(h, 0)].astype(F32)
        for s in (1, 3, 2):
            e_copies[h, o, s].wait_recv()
            total = total + got[o, h, s - 1].astype(F32)
        return total

    h_copies, g_copies = {}, {}

    def back_z(o):
        for h in range(2):
            summed[o, pl.ds(h * 64, 64)] = over_last(h, o).astype(BF)
        for d in (1, 7, 2, 6, 3, 5, 4):
            rows = pl.ds(pl.multiple_of(((z + d) % NZ) * 16, 16), 16)
            h_copies[o, d] = send(
                summed.at[o, rows], got2.at[o, d - 1], h_s.at[o, d - 1], h_r.at[o, d - 1], on_z(d)
            )

    for o in (0, 1, 3, 2):
        if o == 0:
            for h in range(2):
                relay(h, 1)
        for h in range(2):
            for way in range(2):
                if o >= 2 or way != o:
                    b_copies[h, way, o].wait_recv()
            d_copies[h, o].wait_recv()
        unpack(o)
        scores(o)
        give_terms(o)
        if o == 3:
            back_z(0)
        if o == 2:
            back_z(1)
            back_z(3)

    f_copies = []

    def image_rows(k, base, keep):
        cols = slice(base + k * 256, base + (k + 1) * 256)
        for j in range(4):
            lanes = slice(j * 256, (j + 1) * 256)
            keep(k, lanes, dot(coeffs[:, cols], panel[:, lanes], TN))

    def keep_partner(k, lanes, grads):
        igs[k * 256 : (k + 1) * 256, lanes] = grads.astype(BF)

    def keep_mine(k, lanes, grads):
        rows = slice(k * 256, (k + 1) * 256)
        mine[rows, lanes] = (grads + igr[rows, lanes].astype(F32)).astype(BF)

    def my_rows(k):
        f_copies[k].wait_recv()
        image_rows(k, 0, keep_mine)
        rows = pl.ds(k * 256, 256)
        stores.append(load(mine.at[rows], out_images.at[rows], in_sem.at[k]))

    stores = []

    def over_z(o):
        total = summed[o, pl.ds(pl.multiple_of(z * 16, 16), 16)].astype(F32)
        for d in (1, 7, 2, 6, 3, 5, 4):
            h_copies[o, d].wait_recv()
            total = total + got2[o, d - 1].astype(F32)
        return total

    def back_first(o):
        done[o - 1] = over_z(o).astype(BF)
        g_copies[o] = send(
            done.at[o - 1], got1.at[o - 1], g_s.at[o - 1], g_r.at[o - 1], on_own_first(4 - o)
        )

    def partner_rows(k):
        image_rows(k, ROWS, keep_partner)
        rows = pl.ds(k * 256, 256)
        f_copies.append(send(igs.at[rows], igr.at[rows], f_s.at[k], f_r.at[k], partner))

    partner_rows(0)
    partner_rows(1)
    back_z(2)
    partner_rows(2)
    partner_rows(3)
    my_rows(0)
    back_first(1)
    my_rows(1)
    back_first(3)
    my_rows(2)
    my_rows(3)
    back_first(2)
    total = over_z(0)
    for o in (1, 3, 2):
        g_copies[o].wait_recv()
        total = total + got1[o - 1].astype(F32)
    texts_in[:, :HALF] = total[:8]
    texts_in[:, HALF:] = total[8:]
    stores.append(load(texts_in, out_texts, row_sem.at[0]))

    for copy in sends:
        copy.wait_send()
    for copy in stores:
        copy.wait()


def finish(grads, text_grads, out_images, out_texts, low, full, text_low, text_full, in_sem, out_sem):
    loads, stores = [], []
    pieces = [pl.ds(k * 128, 128) for k in range(8)]
    for k, rows in enumerate(pieces):
        loads.append(pltpu.make_async_copy(grads.at[rows], low.at[rows], in_sem.at[k]))
    loads.append(pltpu.make_async_copy(text_grads, text_low, in_sem.at[8]))
    for copy in loads:
        copy.start()
    for k, rows in enumerate(pieces):
        loads[k].wait()
        full[rows] = low[rows].astype(F32) * logit_scale
        stores.append(pltpu.make_async_copy(full.at[rows], out_images.at[rows], out_sem.at[k]))
        stores[k].start()
    loads[8].wait()
    text_full[...] = text_low[...] * logit_scale
    stores.append(pltpu.make_async_copy(text_full, out_texts, out_sem.at[8]))
    stores[8].start()
    for copy in stores:
        copy.wait()


def shards(images, texts, row_lse, row_weights, pair_ids):
    hbm = pl.BlockSpec(memory_space=pltpu.HBM)
    dma = pltpu.SemaphoreType.DMA
    grads, text_grads = pl.pallas_call(
        kernel,
        out_shape=(
            jax.ShapeDtypeStruct((ROWS, D), BF),
            jax.ShapeDtypeStruct((8, D), F32),
        ),
        in_specs=[hbm] * 5,
        out_specs=(hbm, hbm),
        scratch_shapes=[
            pltpu.VMEM((ROWS, D), F32),
            pltpu.VMEM((8, D), F32),
            pltpu.VMEM((2, ROWS), F32),
            pltpu.VMEM((1, ROWS), jnp.int32),
            pltpu.VMEM((2 * ROWS, D), BF),
            pltpu.VMEM((2, 8, ROWS), F32),
            pltpu.VMEM((2, 4, 4, 64, HALF), BF),
            pltpu.VMEM((TEXTS, D), BF),
            pltpu.VMEM((TEXTS, 2 * ROWS), BF),
            pltpu.VMEM((4, 512, HALF), BF),
            pltpu.VMEM((4, 2, 3, 64, HALF), BF),
            pltpu.VMEM((4, 128, HALF), BF),
            pltpu.VMEM((3, 16, HALF), BF),
            pltpu.VMEM((3, 16, HALF), BF),
            pltpu.VMEM((4, 7, 16, HALF), BF),
            pltpu.VMEM((ROWS, D), BF),
            pltpu.VMEM((ROWS, D), BF),
            pltpu.VMEM((ROWS, D), BF),
            dma((4,)), dma((4,)), dma((4,)), dma((4,)), dma, dma, dma((7,)), dma((7,)),
            dma((2, 4)), dma((2, 4)), dma((2, 2, 4)), dma((2, 2, 4)), dma((2, 4)), dma((2, 4)),
            dma((4, 2, 3)), dma((4, 2, 3)), dma((4,)), dma((4,)), dma((3,)), dma((3,)), dma((4, 7)), dma((4, 7)),
        ],
        compiler_params=pltpu.CompilerParams(
            collective_id=0, has_side_effects=True, vmem_limit_bytes=62 * 10**6
        ),
        cost_estimate=pl.CostEstimate(flops=6 * ROWS * 2 * TEXTS * D, bytes_accessed=8 * ROWS * D, transcendentals=2 * ROWS * TEXTS),
        name="tile",
    )(
        images, texts, row_lse.reshape(1, ROWS), row_weights.reshape(1, ROWS), pair_ids.reshape(1, ROWS)
    )
    return pl.pallas_call(
        finish,
        out_shape=(
            jax.ShapeDtypeStruct((ROWS, D), F32),
            jax.ShapeDtypeStruct((8, D), F32),
        ),
        in_specs=[hbm] * 2,
        out_specs=(hbm, hbm),
        scratch_shapes=[
            pltpu.VMEM((ROWS, D), BF),
            pltpu.VMEM((ROWS, D), F32),
            pltpu.VMEM((8, D), F32),
            pltpu.VMEM((8, D), F32),
            dma((9,)),
            dma((9,)),
        ],
        compiler_params=pltpu.CompilerParams(vmem_limit_bytes=62 * 10**6),
        name="finish",
    )(grads, text_grads)


def solution(mesh):
    placed = (
        P(("blk", "group"), None),
        P(("blk", "group"), None),
        P(("blk", "group")),
        P(("blk", "group")),
        P(("blk", "group")),
    )
    return jax.shard_map(
        shards,
        mesh=mesh,
        in_specs=placed,
        out_specs=(P(("blk", "group"), None), P(("blk", "group"), None)),
        check_vma=False,
    )
```

time: 61.4 us -> 59.1 us (0.963); the launches traced: 60.7 us -> 59 us
  Pallas kernels: 54 us -> 58.2 us
  local copies, waits for them, and re-layouts: 3.42 us -> 0 us
  other arithmetic: 2.58 us -> 0 us
    unnamed x9 -> x0, local copies, waits for them, and re-layouts: 3.42 us -> none
    pallas_call x0 -> x1, Pallas kernels: none -> 3.15 us  [shards(): pl.pallas_call(finish, out_shape=(jax.ShapeDtypeStruct((ROWS, D), F32), j...]
    mul x1 -> x0, other arithmetic: 2.58 us -> none  [shards(): return (logit_scale * grads.astype(F32), text_grads)]
    pallas_call x1, Pallas kernels: 54 us -> 55 us  [shards(): pl.pallas_call(kernel, out_shape=(jax.ShapeDtypeStruct((ROWS, D), BF), ja...]
where the time goes in v3:
time: 59.1 us; the launch traced here: 59 us
  Pallas kernels  58.2 us (98%)
  between operations  0.8 us (1%)
    pallas_call x1, Pallas kernels, shards(): pl.pallas_call(kernel, out_shape=(jax.ShapeDtypeStruct((ROWS, D), BF), ja...  55 us
    pallas_call x1, Pallas kernels, shards(): pl.pallas_call(finish, out_shape=(jax.ShapeDtypeStruct((ROWS, D), F32), j...  3.15 us

profile of v3, /device:TPU:8, one launch (start us, length us, event | category | flops | bytes accessed | tf_op | source)
XLA Modules:
  0.0 59.0 jit_solution(6102252298076236149)
XLA Ops:
  0.6 55.0 %tile.1 = (bf16[1024,1024]{1,0:T(8,128)(2,1)}, f32[8,1024]{1,0:T(8,128)}) custom-call(f32[1024,1024]{1,0:T(8,128)} %images.1, f32[8,1024]{1,0:T(8,128)} %texts.1, f32[1,1024]{1,0:T(1,128)} %bitcast.3, f32[1,1024]{1,0:T(1,128)} %bitcast.4, s32[1,1024]{1,0:T(1,128)} %bitcast.5), custom_call_target="tpu_custom_call" | custom-call | flops 12884901888 | bytes 8388608 | tf_op jit(solution)/shard_map/tile/pallas_call | solution.py:332
  55.7 3.1 %finish.1 = (f32[1024,1024]{1,0:T(8,128)}, f32[8,1024]{1,0:T(8,128)}) custom-call(bf16[1024,1024]{1,0:T(8,128)(2,1)} %get-tuple-element.4.grads, f32[8,1024]{1,0:T(8,128)} %get-tuple-element.5.text_grads), custom_call_target="tpu_custom_call" | custom-call | tf_op jit(solution)/shard_map/finish/pallas_call | solution.py:371

commit v4 on v3

--- a/solution.py
+++ b/solution.py
@@ -114,6 +114,10 @@
         loads[k].wait()
         held[rows] = stage[rows].astype(BF)
 
+    core_copies = []
+    for k in range(4):
+        rows, there = pl.ds(k * 256, 256), pl.ds(ROWS + k * 256, 256)
+        core_copies.append(send(held.at[rows], held.at[there], core_s.at[k], core_r.at[k], partner))
     for copy in z_copies:
         copy.wait_recv()
 
@@ -140,10 +144,6 @@
             a_copies[h, o] = send(blob, blob, a_s.at[h, o], a_r.at[h, o], on_first(h, o))
     for h in range(2):
         to_last(h, 0)
-    core_copies = []
-    for k in range(4):
-        rows, there = pl.ds(k * 256, 256), pl.ds(ROWS + k * 256, 256)
-        core_copies.append(send(held.at[rows], held.at[there], core_s.at[k], core_r.at[k], partner))
     for o in (1, 3, 2):
         for h in range(2):
             a_copies[h, o].wait_recv()

time: 59.1 us -> 59.1 us (level)
  no operation moved by 1% of the time
where the time goes in v4:
time: 59.1 us; the launch traced here: 59 us
  Pallas kernels  58.2 us (98%)
  between operations  0.8 us (1%)
    pallas_call x1, Pallas kernels, shards(): pl.pallas_call(kernel, out_shape=(jax.ShapeDtypeStruct((ROWS, D), BF), ja...  55 us
    pallas_call x1, Pallas kernels, shards(): pl.pallas_call(finish, out_shape=(jax.ShapeDtypeStruct((ROWS, D), F32), j...  3.15 us

profile of v4, /device:TPU:8, one launch (start us, length us, event | category | flops | bytes accessed | tf_op | source)
XLA Modules:
  0.0 59.0 jit_solution(977287821298214706)
XLA Ops:
  0.6 55.0 %tile.1 = (bf16[1024,1024]{1,0:T(8,128)(2,1)}, f32[8,1024]{1,0:T(8,128)}) custom-call(f32[1024,1024]{1,0:T(8,128)} %images.1, f32[8,1024]{1,0:T(8,128)} %texts.1, f32[1,1024]{1,0:T(1,128)} %bitcast.3, f32[1,1024]{1,0:T(1,128)} %bitcast.4, s32[1,1024]{1,0:T(1,128)} %bitcast.5), custom_call_target="tpu_custom_call" | custom-call | flops 12884901888 | bytes 8388608 | tf_op jit(solution)/shard_map/tile/pallas_call | solution.py:332
  55.7 3.1 %finish.1 = (f32[1024,1024]{1,0:T(8,128)}, f32[8,1024]{1,0:T(8,128)}) custom-call(bf16[1024,1024]{1,0:T(8,128)(2,1)} %get-tuple-element.4.grads, f32[8,1024]{1,0:T(8,128)} %get-tuple-element.5.text_grads), custom_call_target="tpu_custom_call" | custom-call | tf_op jit(solution)/shard_map/finish/pallas_call | solution.py:371
